TPU v7x, 32 devices: a whole 2x2x4 slice. The times are simulated.
32 devices in a mesh: gx: 8 (over z, core), gy: 4 (over y, x).
Axes of the slice: x: 2, y: 2, z: 4, core: 2. Of those that a mesh axis runs over, the one named last changes fastest.
Arguments:
- bottom_in: bfloat16 [8192, 256], P(('gx', 'gy')), may hold values from -6 to 6
- bottom_pre: bfloat16 [8192, 128], P(('gx', 'gy')), may hold values from -6 to 6
- pooled: bfloat16 [8192, 2, 128], P(('gx', 'gy')), may hold values from -6 to 6
- top_pre: bfloat16 [8192, 1024], P(('gx', 'gy')), may hold values from -6 to 6
- top_cotangent: bfloat16 [8192, 1024], P(('gx', 'gy')), may hold values from -0.375 to 0.375
- top_weight: bfloat16 [384, 1024], replicated, may hold values from -0.5 to 0.5
- lookup_owner: int32 [8192, 2, 32], P(('gx', 'gy')), may hold values from 0 to 31, as said below
- lookup_row: int32 [8192, 2, 32], P(('gx', 'gy')), may hold values from 0 to 2047
Outputs:
- table_grad: float32 [2, 65536, 128], P(None, ('gx', 'gy'))
- top_weight_grad: float32 [384, 1024], P('gy')
- top_bias_grad: float32 [1024], P('gy')
- bottom_weight_grad: float32 [256, 128], P('gy')
Inputs may be any that keep to these rules, and one draw needn't show every extreme that they name: `lookup_owner`: row r of a table with r = owner * 2048 + row is held by device owner in the order of gx+gy. Among the lookups of one device's 256 bags and one table, every owner number appears at most 512 times, and one owner number, the same for all devices of that table, exactly 512 times.
All inputs are finite; a program needn't handle non-finite values.
Results may differ from a plain program's by a relative error of at most 0.003.
Values may be sent and summed in bfloat16 or wider, within the bound.
A program may use at most 128 MiB of HBM per device.

v0:
```python
import math

import jax
import jax.numpy as jnp
from jax import lax
from jax.sharding import PartitionSpec as P

ROWS_DEV = 2048


def slot_positions(owner_lists, devices):
    tables, lookups = owner_lists.shape
    member = (
        owner_lists[:, :, None] == jnp.arange(devices, dtype=jnp.int32)[None, None, :]
    ).astype(jnp.bfloat16)
    block = math.gcd(lookups, 512)
    blocks = lookups // block
    member_blocks = member.reshape(tables, blocks, block, devices)
    lower = (
        jnp.arange(block, dtype=jnp.int32)[:, None] > jnp.arange(block, dtype=jnp.int32)[None, :]
    ).astype(jnp.bfloat16)
    within = jnp.einsum("ik,tnkv->tniv", lower, member_blocks, preferred_element_type=jnp.float32)
    member_float = member_blocks.astype(jnp.float32)
    totals = jnp.sum(member_float, axis=2)
    offsets = jnp.cumsum(totals, axis=1) - totals
    before = within + offsets[:, :, None, :]
    return jnp.sum(before * member_float, axis=3).reshape(tables, lookups).astype(jnp.int32)


def shards(
    bottom_in, bottom_pre, pooled, top_pre, top_cotangent, top_weight, lookup_owner, lookup_row
):
    bag_count = bottom_in.shape[0]
    tables = pooled.shape[1]
    feature_width = pooled.shape[2]
    bag_size = lookup_owner.shape[2]
    top_grad = jnp.where(top_pre > 0, top_cotangent, jnp.zeros_like(top_cotangent))
    bottom_out = jnp.maximum(bottom_pre, jnp.zeros_like(bottom_pre))
    feature = jnp.concatenate(
        [bottom_out, pooled.reshape(bag_count, tables * feature_width)], axis=1
    )
    top_weight_part = lax.dot_general(
        feature, top_grad, (((0,), (0,)), ((), ())), preferred_element_type=jnp.float32
    )
    top_bias_part = jnp.sum(top_grad.astype(jnp.float32), axis=0)
    feature_grad = lax.dot_general(
        top_grad, top_weight, (((1,), (1,)), ((), ())), preferred_element_type=jnp.float32
    ).astype(jnp.bfloat16)
    bottom_grad = jnp.where(
        bottom_pre > 0, feature_grad[:, :feature_width], jnp.zeros_like(bottom_pre)
    )
    bottom_weight_part = lax.dot_general(
        bottom_in, bottom_grad, (((0,), (0,)), ((), ())), preferred_element_type=jnp.float32
    )
    bag_grad = feature_grad[:, feature_width:].reshape(bag_count, tables, feature_width)
    gx_count = lax.axis_size("gx")
    gy_count = lax.axis_size("gy")
    devices = gx_count * gy_count
    capacity = max(2, 2 * bag_count * bag_size // devices)
    local_rows = ROWS_DEV
    slot_total = devices * capacity
    owner_lists = lookup_owner.transpose(1, 0, 2).reshape(tables, bag_count * bag_size)
    positions = slot_positions(owner_lists, devices)
    slot_keys = owner_lists * capacity + positions
    table_index = jnp.broadcast_to(jnp.arange(tables, dtype=jnp.int32)[:, None], slot_keys.shape)
    values = jnp.broadcast_to(
        bag_grad.transpose(1, 0, 2)[:, :, None, :], (tables, bag_count, bag_size, feature_width)
    )
    values = values.reshape(tables, bag_count * bag_size, feature_width)
    row_values = lookup_row.transpose(1, 0, 2).reshape(tables, bag_count * bag_size)
    outgoing = (
        jnp.zeros((slot_total, tables, feature_width), jnp.bfloat16)
        .at[slot_keys, table_index]
        .set(values)
    )
    outgoing_rows = (
        jnp.full((slot_total, tables), local_rows, jnp.int32)
        .at[slot_keys, table_index]
        .set(row_values)
    )
    outgoing = outgoing.reshape(gx_count, gy_count, capacity, tables, feature_width)
    outgoing_rows = outgoing_rows.reshape(gx_count, gy_count, capacity, tables)
    incoming, incoming_rows = (
        lax.all_to_all(
            lax.all_to_all(outgoing, "gx", split_axis=0, concat_axis=0, tiled=True),
            "gy",
            split_axis=1,
            concat_axis=1,
            tiled=True,
        ),
        lax.all_to_all(
            lax.all_to_all(outgoing_rows, "gx", split_axis=0, concat_axis=0, tiled=True),
            "gy",
            split_axis=1,
            concat_axis=1,
            tiled=True,
        ),
    )
    incoming = incoming.reshape(slot_total, tables, feature_width)
    incoming_rows = incoming_rows.reshape(slot_total, tables)
    receive_tables = jnp.broadcast_to(
        jnp.arange(tables, dtype=jnp.int32)[None, :], incoming_rows.shape
    )
    padded_grad = jnp.zeros((tables, local_rows + 1, feature_width), jnp.float32)
    padded_grad = padded_grad.at[receive_tables, incoming_rows].add(incoming.astype(jnp.float32))
    table_grad = padded_grad[:, :local_rows, :]
    shares = (
        lax.psum_scatter(top_weight_part, "gy", scatter_dimension=0, tiled=True),
        lax.psum_scatter(top_bias_part, "gy", scatter_dimension=0, tiled=True),
        lax.psum_scatter(bottom_weight_part, "gy", scatter_dimension=0, tiled=True),
    )
    top_weight_grad, top_bias_grad, bottom_weight_grad = lax.psum(
        (shares[0], shares[1], shares[2]), "gx"
    )
    return (table_grad, top_weight_grad, top_bias_grad, bottom_weight_grad)


def solution(mesh):
    return jax.shard_map(
        shards,
        mesh=mesh,
        in_specs=(
            P(("gx", "gy"), None),
            P(("gx", "gy"), None),
            P(("gx", "gy"), None, None),
            P(("gx", "gy"), None),
            P(("gx", "gy"), None),
            P(),
            P(("gx", "gy"), None, None),
            P(("gx", "gy"), None, None),
        ),
        out_specs=(P(None, ("gx", "gy"), None), P("gy", None), P("gy"), P("gy", None)),
        check_vma=False,
    )
```

profile of v0, /device:TPU:0, one launch (start us, length us, event | category | flops | bytes accessed | tf_op | source)
XLA Modules:
  0.0 679.4 jit_solution(236125855688354416)
XLA Ops:
  7.2 0.0 copy-start
  7.2 0.0 copy-start.12
  7.2 0.0 copy-start.10
  7.2 0.0 copy-start.11
  7.2 0.9 broadcast_multiply_fusion
  8.1 1.0 copy.43
  9.1 0.1 eq.17
  9.3 0.3 convert_reduce_fusion
  9.6 1.0 fusion.2
  10.7 0.1 convert_element_type.36
  10.7 0.1 copy.42
  10.9 0.2 mul.21
  11.0 0.1 compare_select_fusion.2
  11.1 0.2 and_reduce_fusion.1
  11.3 0.2 multiply_reduce_fusion.1
  11.6 0.1 select_bitcast_fusion
  11.7 0.1 copy.44
  11.8 0.1 reshape.158
  11.9 60.4 %scatter_custom_fusion = s32[32768]{0:T(1024)S(1)} fusion(s32[16384]{0:T(1024)S(1)} %bitcast.47, s32[16384]{0:T(1024)S(1)} %reshape.158, s32[]{:T(128)} %constant.8.clone.1), kind=kCustom, calls=%fused_computation.37 | custom fusion | bytes 131076
  72.3 0.1 reshape.144
  72.4 0.1 reshape.136
  72.5 12.9 %all_to_all.20 = s32[8,4,512,2]{2,1,3,0:T(4,128)S(1)} all-to-all(s32[8,4,512,2]{2,1,3,0:T(4,128)S(1)} %copy.45), channel_id=1, replica_groups=mesh['gx'=8,'gy'=4] {'gx'}, dimensions={0} | all-to-all | bytes 262144 | tf_op jit(solution)/shard_map/all_to_all | solution.py:92
  85.5 0.7 copy.46
  86.2 3.7 all-to-all-start.1
  89.9 0.5 convolution_convert_fusion
  90.5 2.5 broadcast_in_dim.17
  92.9 46.2 %scatter_custom_fusion.1 = bf16[32768,128]{1,0:T(8,128)(2,1)} fusion(s32[16384]{0:T(1024)S(1)} %bitcast.46, bf16[16384,128]{1,0:T(8,128)(2,1)} %bitcast.39, bf16[]{:T(256)} %constant.13.clone.1), kind=kCustom, calls=%fused_computation.4 | custom fusion | bytes 8389120
  139.2 5.1 all-to-all-start.2
  144.3 0.0 reduce-scatter.7.cloned.1.call-start
  144.4 0.2 convolution_bitcast_fusion
  144.6 0.8 copy.56
  145.4 0.0 reduce-scatter.7.cloned.1.call-update
  145.4 0.2 reduce-scatter.5.cloned.1.call-start
  145.7 1.5 fusion.10
  147.2 0.0 reduce-scatter.5.cloned.1.call-update
  147.2 0.6 dynamic-slice
  148.5 0.2 convert_reduce_fusion.1
  148.7 10.4 %all-reduce = f32[1024]{0:T(1024)S(1)} all-reduce(f32[1024]{0:T(1024)S(1)} %convert_reduce_fusion.1), channel_id=3, replica_groups=mesh['gx'=8,'gy'=4] {'gy'}, use_global_device_ids=true, to_apply=%region_9.10.clone | all-reduce | flops 1024 | bytes 8192
  159.1 0.1 dynamic-slice.1
  159.2 15.0 %reduce-scatter.7.cloned.1.call-done = f32[64,128]{1,0:T(8,128)} async-done(((f32[256,128]{1,0:T(8,128)}), f32[64,128]{1,0:T(8,128)}) %reduce-scatter.7.cloned.1.call-update) | async-done | bytes 32784
  174.2 0.8 copy.57
  175.0 169.2 %all-reduce.1 = (f32[256]{0:T(256)}, f32[64,128]{0,1:T(8,128)S(1)}) all-reduce(f32[256]{0:T(256)S(1)} %dynamic-slice.1, f32[64,128]{0,1:T(8,128)S(1)} %copy.57), channel_id=1, replica_groups=mesh['gx'=8,'gy'=4] {'gx'}, use_global_device_ids=true, to_apply=%region_10.11 | all-reduce | flops 8448 | bytes 67584 | tf_op jit(solution)/shard_map/psum | solution.py:112
  344.2 0.7 copy.54
  344.9 0.1 copy.47
  345.0 0.1 reshape.137
  345.2 8.2 %copy.50 = bf16[8,4,512,2,128]{4,3,2,0,1:T(2,128)(2,1)} copy(bf16[8,4,512,2,128]{4,3,2,1,0:T(2,128)(2,1)} %all-to-all-done.2) | data formatting | bytes 16777216 | tf_op jit(solution)/shard_map/all_to_all | solution.py:85
  353.3 5.8 all-to-all-start.3
  359.1 0.0 all-reduce.4.cloned.1.call-start
  359.2 0.1 compare_select_fusion.1
  359.3 0.2 multiply_reduce_fusion
  359.5 0.3 and_reduce_fusion
  359.9 0.1 broadcast_select_fusion
  360.0 5.0 copy.48
  365.0 6.9 %reshape.168 = s32[32768]{0:T(1024)S(1)} reshape(s32[16384,2]{1,0:T(8,128)} %copy.48) | data formatting | bytes 262144
  371.9 0.0 reduce-scatter.5.cloned.1.call-done
  371.9 0.0 all-reduce.4.cloned.1.call-update
  371.9 79.0 %all-to-all-done.3 = bf16[8,4,512,2,128]{4,3,2,0,1:T(2,128)(2,1)} async-done(((bf16[8,4,512,2,128]{4,3,2,0,1:T(2,128)(2,1)}), bf16[8,4,512,2,128]{4,3,2,0,1:T(2,128)(2,1)}, u32[]{:S(2)}, u32[]{:S(2)}) %all-to-all-start.3) | async-done | bytes 8388640 | tf_op jit(solution)/shard_map/all_to_all | solution.py:84
  450.9 11.1 %copy_convert_fusion = f32[8,4,512,2,128]{4,2,3,1,0:T(8,128)} fusion(bf16[8,4,512,2,128]{4,3,2,0,1:T(2,128)(2,1)} %all-to-all-done.3), kind=kLoop, calls=%fused_computation.3 | loop fusion | flops 4194304 | bytes 25165824 | tf_op jit(solution)/shard_map/convert_element_type | solution.py:105
  462.0 28.5 %copy.52 = f32[8,4,512,2,128]{4,3,2,1,0:T(2,128)} copy(f32[8,4,512,2,128]{4,2,3,1,0:T(8,128)} %copy_convert_fusion) | data formatting | bytes 33554432 | tf_op jit(solution)/shard_map/convert_element_type | solution.py:105
  490.6 174.7 %scatter_custom_fusion.2 = f32[4098,128]{1,0:T(8,128)S(1)} fusion(s32[32768]{0:T(1024)S(1)} %reshape.168, f32[32768,128]{1,0:T(8,128)} %bitcast.37, f32[]{:T(128)} %constant.7.clone.1), kind=kCustom, calls=%fused_computation.14 | custom fusion | flops 4194304 | bytes 2098688
  665.3 2.6 reshape.152
  667.9 1.7 slice.13
  669.6 1.5 copy.53
  671.1 1.8 copy.65
  (40 shorter events, 0.3 us)
Async XLA Ops:
  7.2 82.7 %copy-start = (bf16[384,1024]{1,0:T(8,128)(2,1)S(1)}, bf16[384,1024]{1,0:T(8,128)(2,1)}, u32[]{:S(2)}) copy-start(bf16[384,1024]{1,0:T(8,128)(2,1)} %param.13) | copy-start | bytes 2359300
  7.2 3.9 copy-start.12
  7.2 4.1 copy-start.10
  7.2 4.1 copy-start.11
  7.2 4.5 copy-start.7
  9.6 80.3 %copy-start.2 = (bf16[256,1024]{1,0:T(8,128)(2,1)S(1)}, bf16[256,1024]{1,0:T(8,128)(2,1)}, u32[]{:S(2)}) copy-start(bf16[256,1024]{1,0:T(8,128)(2,1)} %param.12) | copy-start | bytes 1572868
  9.6 80.3 %copy-start.3 = (bf16[256,1024]{1,0:T(8,128)(2,1)S(1)}, bf16[256,1024]{1,0:T(8,128)(2,1)}, u32[]{:S(2)}) copy-start(bf16[256,1024]{1,0:T(8,128)(2,1)} %param.11) | copy-start | bytes 1572868
  86.2 53.0 %all-to-all-start.1 = ((s32[8,4,512,2]{2,0,3,1:T(8,128)}), s32[8,4,512,2]{2,0,3,1:T(8,128)S(1)}, u32[]{:S(2)}, u32[]{:S(2)}) async-start(s32[8,4,512,2]{2,0,3,1:T(8,128)} %copy.46), calls=%async_computation.1 | async-start | bytes 262144 | tf_op jit(solution)/shard_map/all_to_all | solution.py:91
  139.2 5.2 copy-start.4
  139.2 5.2 copy-start.5
  139.2 6.4 copy-start.6
  139.2 205.9 %all-to-all-start.2 = ((bf16[8,4,512,2,128]{4,3,2,1,0:T(2,128)(2,1)}), bf16[8,4,512,2,128]{4,3,2,1,0:T(2,128)(2,1)}, u32[]{:S(2)}, u32[]{:S(2)}) async-start(bf16[8,4,512,2,128]{4,3,2,1,0:T(2,128)(2,1)} %bitcast.36), calls=%async_computation.2 | async-start | bytes 16777216 | tf_op jit(solution)/shard_map/all_to_all | solution.py:85
  144.3 2.9 copy-start.13
  144.3 29.9 %reduce-scatter.7.cloned.1.call-start = ((), (), s32[]{:S(2)}) async-start(), calls=%async_computation.8 | async-start | bytes 163840
  145.4 226.5 %reduce-scatter.5.cloned.1.call-start = ((), (), s32[]{:S(2)}) async-start(), calls=%async_computation.6 | async-start | bytes 1966080 | tf_op jit(solution)/shard_map/reduce_scatter | solution.py:108
  353.3 6.0 copy-start.9
  353.3 6.2 copy-start.8
  353.3 97.5 %all-to-all-start.3 = ((bf16[8,4,512,2,128]{4,3,2,0,1:T(2,128)(2,1)}), bf16[8,4,512,2,128]{4,3,2,0,1:T(2,128)(2,1)}, u32[]{:S(2)}, u32[]{:S(2)}) async-start(bf16[8,4,512,2,128]{4,3,2,0,1:T(2,128)(2,1)} %copy.50), calls=%async_computation.3 | async-start | bytes 16777216 | tf_op jit(solution)/shard_map/all_to_all | solution.py:84
  359.1 311.9 %all-reduce.4.cloned.1.call-start = ((), (), s32[]{:S(2)}) async-start(), calls=%async_computation.7 | async-start | bytes 786432 | tf_op jit(solution)/shard_map/psum | solution.py:112
  667.9 4.9 copy-start.1
Sparse Core Ops, SparseCore 0:
  148.5 25.6 reduce-scatter.6
  178.0 30.9 reduce-scatter.4
  372.0 55.5 all-reduce.3
where the time goes:
time: 680 us; the launch traced here: 679 us
  blocking collectives  193 us (28%)
  other arithmetic  189 us (28%)
  local copies, waits for them, and re-layouts  171 us (25%)
  waiting for transfers between devices  94 us (14%)
  starting transfers between devices  14.9 us (2%)
  between operations  14.9 us (2%)
    unnamed x7, other arithmetic  176 us
    psum x1, blocking collectives, shards(): lax.psum((shares[0], shares[1], shares[2]), 'gx')  169 us
    unnamed x44, local copies, waits for them, and re-layouts  127 us
    all_to_all x1, waiting for transfers between devices, shards(): lax.all_to_all(lax.all_to_all(outgoing, 'gx', split_axis=0, concat_axis=0...  79 us
    convert_element_type x1, local copies, waits for them, and re-layouts, shards(): incoming.astype(jnp.float32)  28.5 us
    unnamed x4, waiting for transfers between devices  15.1 us
  transfers between devices with their start and end apart: 6, of which 2 were waited for; matrix products, arithmetic and copies ran while one was open for 43% of the time, Pallas kernels for 0%

commit v1 on v0

v1 whole, which is shorter than its diff:
```python
import functools

import jax
import jax.numpy as jnp
from jax import lax
from jax.experimental import pallas as pl
from jax.experimental.pallas import tpu as pltpu
from jax.sharding import PartitionSpec as P

ROWS_DEV = 2048
LOW = 256
BAG_STEP = 4096
ROW_BLOCK = 512
AXES = ("gx", "gy")


def one_hot(condition):
    return jnp.where(condition, 1.0, 0.0).astype(jnp.bfloat16)


def pack_kernel(devices, capacity, tables, owner_ref, row_ref, codes_ref):
    lists, bags = owner_ref.shape
    bag_size = lists // tables
    f32 = jnp.float32
    earlier = one_hot(
        lax.broadcasted_iota(jnp.int32, (bags, bags), 0)
        < lax.broadcasted_iota(jnp.int32, (bags, bags), 1)
    )
    owner_ids = lax.broadcasted_iota(jnp.int32, (devices, bags), 0)
    slot_ids = lax.broadcasted_iota(jnp.int32, (capacity, bags), 0)
    bag_ids = lax.broadcasted_iota(jnp.int32, (1, bags), 1).astype(f32)
    for table in range(tables):
        carry = jnp.zeros((devices, 1), f32)
        total = jnp.zeros((3 * devices, capacity), f32)
        for item in range(bag_size):
            at = table * bag_size + item
            owner = owner_ref[at : at + 1, :]
            row = row_ref[at : at + 1, :] + LOW
            hit = owner == owner_ids
            member = jnp.where(hit, 1.0, 0.0)
            before = lax.dot_general(
                member.astype(jnp.bfloat16),
                earlier,
                (((1,), (0,)), ((), ())),
                preferred_element_type=f32,
            )
            slot = jnp.sum(member * (before + carry), axis=0, keepdims=True)
            carry = carry + jnp.sum(member, axis=1, keepdims=True)
            high = (row // LOW).astype(f32)
            low = (row % LOW).astype(f32)
            left = jnp.concatenate(
                [member * bag_ids, member * high, member * low], axis=0
            ).astype(jnp.bfloat16)
            right = one_hot(slot.astype(jnp.int32) == slot_ids)
            total = total + lax.dot_general(
                left, right, (((1,), (1,)), ((), ())), preferred_element_type=f32
            )
        code = total[:devices] * BAG_STEP + total[devices : 2 * devices] * LOW + total[2 * devices :]
        codes_ref[:, table * capacity : (table + 1) * capacity] = code.astype(jnp.int32)


def add_kernel(capacity, tables, bags, width, sub, codes_ref, grads_ref, out_ref):
    f32 = jnp.float32
    group = codes_ref.shape[1]
    local_rows = out_ref.shape[1]
    parts = local_rows // ROW_BLOCK

    @pl.when(pl.program_id(0) == 0)
    def _():
        out_ref[...] = jnp.zeros_like(out_ref)

    codes = codes_ref[0]
    columns = jnp.transpose(codes)
    bag_ids = lax.broadcasted_iota(jnp.int32, (capacity, bags), 1)
    row_ids = lax.broadcasted_iota(jnp.int32, (ROW_BLOCK, capacity), 0)
    for table in range(tables):
        for first in range(0, group, sub):
            lefts, rights = [], []
            for source in range(first, first + sub):
                spot = slice(table * capacity, (table + 1) * capacity)
                line = codes[source : source + 1, spot] % BAG_STEP - LOW
                lefts.append(one_hot((line & (ROW_BLOCK - 1)) == row_ids))
                column = columns[spot, source : source + 1]
                picked = lax.dot_general(
                    one_hot((column // BAG_STEP) == bag_ids),
                    grads_ref[source * bags : (source + 1) * bags, table * width : (table + 1) * width],
                    (((1,), (0,)), ((), ())),
                    preferred_element_type=f32,
                )
                part = jnp.broadcast_to((column % BAG_STEP - LOW) // ROW_BLOCK, picked.shape)
                rights.append(
                    jnp.concatenate(
                        [jnp.where(part == p, picked, 0.0).astype(jnp.bfloat16) for p in range(parts)],
                        axis=1,
                    )
                )
            result = lax.dot_general(
                jnp.concatenate(lefts, axis=1),
                jnp.concatenate(rights, axis=0),
                (((1,), (0,)), ((), ())),
                preferred_element_type=f32,
            )
            for p in range(parts):
                out_ref[table, p * ROW_BLOCK : (p + 1) * ROW_BLOCK, :] += result[
                    :, p * width : (p + 1) * width
                ]


def pack_codes(owner_lists, row_lists, devices, capacity, tables):
    return pl.pallas_call(
        functools.partial(pack_kernel, devices, capacity, tables),
        out_shape=jax.ShapeDtypeStruct((devices, tables * capacity), jnp.int32),
        in_specs=[pl.BlockSpec(memory_space=pltpu.VMEM)] * 2,
        out_specs=pl.BlockSpec(memory_space=pltpu.VMEM),
        compiler_params=pltpu.CompilerParams(vmem_limit_bytes=32 * 2**20),
        cost_estimate=pl.CostEstimate(flops=2 * 10**9, bytes_accessed=10**6, transcendentals=0),
        name="pack",
    )(owner_lists, row_lists)


def add_rows(codes, grads, capacity, tables, bags, width, local_rows):
    sources = codes.shape[0]
    group = 8
    steps = sources // group
    return pl.pallas_call(
        functools.partial(add_kernel, capacity, tables, bags, width, 4),
        grid=(steps,),
        out_shape=jax.ShapeDtypeStruct((tables, local_rows, width), jnp.float32),
        in_specs=[
            pl.BlockSpec((1, group, tables * capacity), lambda i: (i, 0, 0)),
            pl.BlockSpec((group * bags, tables * width), lambda i: (i, 0)),
        ],
        out_specs=pl.BlockSpec((tables, local_rows, width), lambda i: (0, 0, 0)),
        compiler_params=pltpu.CompilerParams(vmem_limit_bytes=48 * 2**20),
        cost_estimate=pl.CostEstimate(flops=40 * 10**9, bytes_accessed=8 * 10**6, transcendentals=0),
        name="add_rows",
    )(codes.reshape(steps, group, tables * capacity), grads)


def shards(
    bottom_in, bottom_pre, pooled, top_pre, top_cotangent, top_weight, lookup_owner, lookup_row
):
    bags = bottom_in.shape[0]
    tables = pooled.shape[1]
    width = pooled.shape[2]
    bag_size = lookup_owner.shape[2]
    devices = lax.axis_size("gx") * lax.axis_size("gy")
    capacity = max(2, 2 * bags * bag_size // devices)
    top_grad = jnp.where(top_pre > 0, top_cotangent, jnp.zeros_like(top_cotangent))
    feature_grad = lax.dot_general(
        top_grad, top_weight, (((1,), (1,)), ((), ())), preferred_element_type=jnp.float32
    ).astype(jnp.bfloat16)
    grads = lax.all_gather(feature_grad[:, width:], AXES, axis=0, tiled=True)
    owner_lists = lookup_owner.reshape(bags, tables * bag_size).T
    row_lists = lookup_row.reshape(bags, tables * bag_size).T
    codes = pack_codes(owner_lists, row_lists, devices, capacity, tables)
    codes = lax.all_to_all(codes, AXES, split_axis=0, concat_axis=0, tiled=True)
    bottom_out = jnp.maximum(bottom_pre, jnp.zeros_like(bottom_pre))
    feature = jnp.concatenate([bottom_out, pooled.reshape(bags, tables * width)], axis=1)
    top_weight_part = lax.dot_general(
        feature, top_grad, (((0,), (0,)), ((), ())), preferred_element_type=jnp.float32
    )
    top_bias_part = jnp.sum(top_grad.astype(jnp.float32), axis=0)
    bottom_grad = jnp.where(bottom_pre > 0, feature_grad[:, :width], jnp.zeros_like(bottom_pre))
    bottom_weight_part = lax.dot_general(
        bottom_in, bottom_grad, (((0,), (0,)), ((), ())), preferred_element_type=jnp.float32
    )
    shares = (
        lax.psum_scatter(top_weight_part, "gy", scatter_dimension=0, tiled=True),
        lax.psum_scatter(top_bias_part, "gy", scatter_dimension=0, tiled=True),
        lax.psum_scatter(bottom_weight_part, "gy", scatter_dimension=0, tiled=True),
    )
    top_weight_grad, top_bias_grad, bottom_weight_grad = lax.psum(shares, "gx")
    table_grad = add_rows(codes, grads, capacity, tables, bags, width, ROWS_DEV)
    return (table_grad, top_weight_grad, top_bias_grad, bottom_weight_grad)


def solution(mesh):
    return jax.shard_map(
        shards,
        mesh=mesh,
        in_specs=(
            P(AXES, None),
            P(AXES, None),
            P(AXES, None, None),
            P(AXES, None),
            P(AXES, None),
            P(),
            P(AXES, None, None),
            P(AXES, None, None),
        ),
        out_specs=(P(None, AXES, None), P("gy", None), P("gy"), P("gy", None)),
        check_vma=False,
    )
```

time: 680 us -> 146 us (0.21)
  other arithmetic: 189 us -> 0.21 us
  local copies, waits for them, and re-layouts: 171 us -> 9.65 us
  blocking collectives: 193 us -> 39.3 us
  waiting for transfers between devices: 94 us -> 25.7 us
  Pallas kernels: 0 us -> 43.8 us
  starting transfers between devices: 14.9 us -> 7.46 us
    unnamed x7 -> x0, other arithmetic: 176 us -> none
    psum x1, blocking collectives: 169 us -> 29.1 us  [shards(): top_weight_grad, top_bias_grad, bottom_weight_grad = lax.psum(shares, 'gx')]
    unnamed x44 -> x28, local copies, waits for them, and re-layouts: 127 us -> 8.2 us
    all_to_all x3 -> x1, waiting for transfers between devices: 79 us -> 0.01 us  [shards(): codes = lax.all_to_all(codes, AXES, split_axis=0, concat_axis=0, tiled=True)]
    pallas_call x0 -> x2, Pallas kernels: none -> 43.8 us  [the longest x1 28.2 us: add_rows(): pl.pallas_call(functools.partial(add_kernel, capacity, tables, bags, widt...]
    convert_element_type x2 -> x0, local copies, waits for them, and re-layouts: 28.6 us -> none  [the longest x1 28.5 us: shards(): incoming.astype(jnp.float32)]
    psum x1, waiting for transfers between devices: 0.01 us -> 24.1 us  [shards(): top_weight_grad, top_bias_grad, bottom_weight_grad = lax.psum(shares, 'gx')]
    unnamed x4 -> x5, waiting for transfers between devices: 15.1 us -> 0.09 us
  transfers between devices with their start and end apart: 6 -> 5, of which waited for: 2 -> 2; matrix products, arithmetic and copies ran while one was open for 43% -> 4% of each run, Pallas kernels for 0% -> 30%
where the time goes in v1:
time: 146 us
  Pallas kernels  43.8 us (30%)
  blocking collectives  39.3 us (27%)
  waiting for transfers between devices  25.7 us (18%)
  between operations  16 us (11%)
  local copies, waits for them, and re-layouts  9.65 us (7%)
  starting transfers between devices  7.46 us (5%)
  matrix products  3.38 us (2%)
    psum x1, blocking collectives, shards(): top_weight_grad, top_bias_grad, bottom_weight_grad = lax.psum(shares, 'gx')  29.1 us
    pallas_call x1, Pallas kernels, add_rows(): pl.pallas_call(functools.partial(add_kernel, capacity, tables, bags, widt...  28.2 us
    psum x1, waiting for transfers between devices, shards(): top_weight_grad, top_bias_grad, bottom_weight_grad = lax.psum(shares, 'gx')  24.1 us
    pallas_call x1, Pallas kernels, pack_codes(): pl.pallas_call(functools.partial(pack_kernel, devices, capacity, tables),...  15.6 us
    unnamed x1, blocking collectives  10.1 us
    unnamed x28, local copies, waits for them, and re-layouts  8.2 us
    all_to_all x1, starting transfers between devices, shards(): codes = lax.all_to_all(codes, AXES, split_axis=0, concat_axis=0, tiled=True)  7.29 us
  transfers between devices with their start and end apart: 5, of which 2 were waited for; matrix products, arithmetic and copies ran while one was open for 4% of the time, Pallas kernels for 30%

profile of v1, /device:TPU:0, one launch (start us, length us, event | category | flops | bytes accessed | tf_op | source)
XLA Modules:
  0.0 145.5 jit_solution(8735700409057745104)
XLA Ops:
  8.0 0.0 copy-start
  8.0 0.0 copy-start.5
  8.0 0.0 copy-start.4
  8.0 0.0 copy-start.7
  8.0 0.0 copy-start.6
  8.1 0.0 copy-start.8
  8.1 0.0 reduce-scatter.7.cloned.1.call-start
  8.1 1.2 copy-done
  9.3 1.7 %convolution_convert_fusion = bf16[256,384]{1,0:T(8,128)(2,1)S(1)} fusion(bf16[384,1024]{1,0:T(8,128)(2,1)S(1)} %copy-done, bf16[256,1024]{1,0:T(8,128)(2,1)} %param.12, bf16[256,1024]{1,0:T(8,128)(2,1)} %param.11), kind=kOutput, calls=%fused_computation | convolution fusion | flops 201949184 | bytes 2031616 | tf_op jit(solution)/shard_map/dot_general | solution.py:150
  11.0 0.0 copy-done.7
  11.0 0.0 copy-done.6
  11.0 0.2 convolution_bitcast_fusion
  11.2 0.8 copy.15
  11.9 0.0 reduce-scatter.7.cloned.1.call-update
  12.0 0.0 reduce-scatter.5.cloned.1.call-start
  12.0 0.0 copy-done.8
  12.1 0.0 copy-done.5
  12.1 0.0 copy-done.4
  12.1 0.0 copy-start.2
  12.1 0.0 copy-start.3
  12.1 1.5 %fusion = f32[384,1024]{1,0:T(8,128)} fusion(bf16[256,256]{1,0:T(8,128)(2,1)S(1)} %bitcast.24, bf16[256,128]{1,0:T(8,128)(2,1)S(1)} %broadcast_maximum_fusion, bf16[256,1024]{1,0:T(8,128)(2,1)S(1)} %copy-done.4, bf16[256,1024]{1,0:T(8,128)(2,1)S(1)} %copy-done.5), kind=kOutput, calls=%fused_computation.4 | convolution fusion | flops 202244096 | bytes 2818048 | tf_op jit(solution)/shard_map/dot_general | solution.py:160
  13.6 0.0 reduce-scatter.5.cloned.1.call-update
  13.7 0.0 all-gather.2.cloned.1.call-start
  13.7 0.7 slice.8
  14.4 0.0 all-gather.2.cloned.1.call-update
  14.4 0.0 copy-done.2
  14.4 0.0 copy-done.3
  14.4 0.0 copy-start.9
  14.4 15.6 %pack.1 = s32[32,1024]{1,0:T(8,128)S(1)} custom-call(s32[64,256]{1,0:T(8,128)S(1)} %bitcast.22, s32[64,256]{1,0:T(8,128)S(1)} %bitcast.23), custom_call_target="tpu_custom_call" | custom-call | flops 2000000000 | bytes 1000000 | tf_op jit(solution)/shard_map/pack/pallas_call | solution.py:110
  30.0 0.8 copy.13
  30.8 7.3 %all-to-all-start = ((s32[32,1,1024]{2,1,0:T(1,128)}), s32[32,1,1024]{2,1,0:T(1,128)S(1)}, u32[]{:S(2)}, u32[]{:S(2)}) async-start(s32[32,1,1024]{2,1,0:T(1,128)} %copy.13), calls=%async_computation | async-start | bytes 262144 | tf_op jit(solution)/shard_map/all_to_all | solution.py:157
  38.1 0.0 all-reduce.4.cloned.1.call-start
  38.2 0.0 copy-done.9
  38.2 0.6 dynamic-slice
  39.4 0.2 convert_reduce_fusion
  39.6 10.1 %all-reduce = f32[1024]{0:T(1024)S(1)} all-reduce(f32[1024]{0:T(1024)S(1)} %convert_reduce_fusion), channel_id=3, replica_groups=mesh['gx'=8,'gy'=4] {'gy'}, use_global_device_ids=true, to_apply=%region_3.4.clone | all-reduce | flops 1024 | bytes 8192
  49.8 0.1 dynamic-slice.1
  49.9 0.0 all-to-all-done
  49.9 0.0 reduce-scatter.7.cloned.1.call-done
  49.9 0.8 copy.16
  50.8 29.1 %all-reduce.1 = (f32[256]{0:T(256)}, f32[64,128]{0,1:T(8,128)S(1)}) all-reduce(f32[256]{0:T(256)S(1)} %dynamic-slice.1, f32[64,128]{0,1:T(8,128)S(1)} %copy.16), channel_id=1, replica_groups=mesh['gx'=8,'gy'=4] {'gx'}, use_global_device_ids=true, to_apply=%region_4.5 | all-reduce | flops 8448 | bytes 67584 | tf_op jit(solution)/shard_map/psum | solution.py:173
  79.9 0.7 copy.14
  80.6 0.0 reduce-scatter.5.cloned.1.call-done
  80.6 0.0 all-reduce.4.cloned.1.call-update
  80.6 1.5 %all-gather.2.cloned.1.call-done.grads_ref = bf16[8192,256]{1,0:T(8,128)(2,1)} async-done(((bf16[256,256]{1,0:T(8,128)(2,1)}), bf16[8192,256]{1,0:T(8,128)(2,1)}) %all-gather.2.cloned.1.call-update) | async-done | bytes 4194320 | tf_op jit(solution)/shard_map/all_gather | solution.py:153
  82.2 0.0 copy-start.1
  82.2 2.2 %copy-done.1 = bf16[8192,256]{1,0:T(8,128)(2,1)S(1)} copy-done((bf16[8192,256]{1,0:T(8,128)(2,1)S(1)}, bf16[8192,256]{1,0:T(8,128)(2,1)}, u32[]{:S(2)}) %copy-start.1) | copy-done | bytes 4194328
  84.4 28.2 %add_rows.1 = f32[2,2048,128]{2,1,0:T(8,128)} custom-call(s32[4,8,1024]{2,1,0:T(8,128)S(1)} %bitcast.20, bf16[8192,256]{1,0:T(8,128)(2,1)S(1)} %copy-done.1), custom_call_target="tpu_custom_call" | custom-call | flops 40000000000 | bytes 8000000 | tf_op jit(solution)/shard_map/add_rows/pallas_call | solution.py:125
  112.5 24.1 %all-reduce.4.cloned.1.call-done = f32[96,1024]{1,0:T(8,128)} async-done(((f32[96,1024]{1,0:T(8,128)}), f32[96,1024]{1,0:T(8,128)}) %all-reduce.4.cloned.1.call-update) | async-done | bytes 393232 | tf_op jit(solution)/shard_map/psum | solution.py:173
  136.6 1.8 %copy.24 = f32[96,1024]{1,0:T(8,128)} copy(f32[96,1024]{1,0:T(8,128)} %all-reduce.4.cloned.1.call-done) | data formatting | bytes 786432
  (3 shorter events, 0.1 us)
Async XLA Ops:
  8.0 1.3 copy-start
  8.0 4.0 %copy-start.5 = (bf16[256,1024]{1,0:T(8,128)(2,1)S(1)}, bf16[256,1024]{1,0:T(8,128)(2,1)}, u32[]{:S(2)}) copy-start(bf16[256,1024]{1,0:T(8,128)(2,1)} %param.11) | copy-start | bytes 1572868
  8.0 4.0 %copy-start.4 = (bf16[256,1024]{1,0:T(8,128)(2,1)S(1)}, bf16[256,1024]{1,0:T(8,128)(2,1)}, u32[]{:S(2)}) copy-start(bf16[256,1024]{1,0:T(8,128)(2,1)} %param.12) | copy-start | bytes 1572868
  8.0 2.9 %copy-start.7 = (bf16[256,256]{1,0:T(8,128)(2,1)S(1)}, bf16[256,256]{1,0:T(8,128)(2,1)}, u32[]{:S(2)}) copy-start(bf16[256,256]{1,0:T(8,128)(2,1)} %param.8) | copy-start | bytes 393220
  8.0 2.9 %copy-start.6 = (bf16[256,128]{1,0:T(8,128)(2,1)S(1)}, bf16[256,128]{1,0:T(8,128)(2,1)}, u32[]{:S(2)}) copy-start(bf16[256,128]{1,0:T(8,128)(2,1)} %param.9) | copy-start | bytes 196612
  8.1 4.0 %copy-start.8 = (bf16[256,2,128]{2,1,0:T(2,128)(2,1)S(1)}, bf16[256,2,128]{2,1,0:T(2,128)(2,1)}, u32[]{:S(2)}) copy-start(bf16[256,2,128]{2,1,0:T(2,128)(2,1)} %param.10) | copy-start | bytes 393220
  8.1 41.8 %reduce-scatter.7.cloned.1.call-start = ((), (), s32[]{:S(2)}) async-start(), calls=%async_computation.6 | async-start | bytes 163840
  12.0 68.7 %reduce-scatter.5.cloned.1.call-start = ((), (), s32[]{:S(2)}) async-start(), calls=%async_computation.4 | async-start | bytes 1966080 | tf_op jit(solution)/shard_map/reduce_scatter | solution.py:169
  12.1 2.3 %copy-start.2 = (s32[256,2,32]{0,2,1:T(8,128)S(1)}, s32[256,2,32]{0,2,1:T(8,128)}, u32[]{:S(2)}) copy-start(s32[256,2,32]{0,2,1:T(8,128)} %param.14) | copy-start | bytes 196612
  12.1 2.3 %copy-start.3 = (s32[256,2,32]{0,2,1:T(8,128)S(1)}, s32[256,2,32]{0,2,1:T(8,128)}, u32[]{:S(2)}) copy-start(s32[256,2,32]{0,2,1:T(8,128)} %param.15) | copy-start | bytes 196612
  13.7 68.5 %all-gather.2.cloned.1.call-start = ((), (), s32[]{:S(2)}) async-start(), calls=%async_computation.3 | async-start | bytes 4325376 | tf_op jit(solution)/shard_map/all_gather | solution.py:153
  14.4 23.8 %copy-start.9 = (u32[32]{0:T(128)S(1)}, u32[32]{0:T(128)}, u32[]{:S(2)}) copy-start(u32[32]{0:T(128)} %constant.7) | copy-start | bytes 388
  30.8 19.0 %all-to-all-start = ((s32[32,1,1024]{2,1,0:T(1,128)}), s32[32,1,1024]{2,1,0:T(1,128)S(1)}, u32[]{:S(2)}, u32[]{:S(2)}) async-start(s32[32,1,1024]{2,1,0:T(1,128)} %copy.13), calls=%async_computation | async-start | bytes 262144 | tf_op jit(solution)/shard_map/all_to_all | solution.py:157
  38.1 98.5 %all-reduce.4.cloned.1.call-start = ((), (), s32[]{:S(2)}) async-start(), calls=%async_computation.5 | async-start | bytes 786432 | tf_op jit(solution)/shard_map/psum | solution.py:173
  82.2 2.2 %copy-start.1 = (bf16[8192,256]{1,0:T(8,128)(2,1)S(1)}, bf16[8192,256]{1,0:T(8,128)(2,1)}, u32[]{:S(2)}) copy-start(bf16[8192,256]{1,0:T(8,128)(2,1)} %all-gather.2.cloned.1.call-done.grads_ref) | copy-start | bytes 12582916
Sparse Core Ops, SparseCore 0:
  12.1 26.7 reduce-scatter.6
  42.7 35.7 reduce-scatter.4
  80.9 55.6 all-reduce.3
Sparse Core Ops, SparseCore 1:
  17.0 65.1 all-gather.1

commit v2 on v1

--- a/solution.py
+++ b/solution.py
@@ -18,10 +18,96 @@
     return jnp.where(condition, 1.0, 0.0).astype(jnp.bfloat16)
 
 
-def pack_kernel(devices, capacity, tables, owner_ref, row_ref, codes_ref):
-    lists, bags = owner_ref.shape
-    bag_size = lists // tables
+def exchange_kernel(
+    gx_count, gy_count, capacity, tables,
+    owner_ref, row_ref, own_ref, part_ref,
+    grads_ref, codes_ref, sums_ref,
+    lists, outgoing, pair_in, pair_sum, plane_in, plane_sum, line_in,
+    keep_sem, line_send, plane_send, core_send, block_recv, code_send, code_recv,
+    pair_sems, plane_sum_send, plane_sum_recv, line_sum_send, line_sum_recv,
+    back_send, back_core_send, back_recv,
+):
+    chips = gx_count // 2
+    devices = gx_count * gy_count
+    gx, gy = lax.axis_index("gx"), lax.axis_index("gy")
+    me = gx * gy_count + gy
+    z, core = gx // 2, gx % 2
+    sibling = (z * 2 + 1 - core, gy)
+    bags = own_ref.shape[0]
     f32 = jnp.float32
+
+    def remote(source, target, send, recv, device):
+        return pltpu.make_async_remote_copy(
+            src_ref=source,
+            dst_ref=target,
+            send_sem=send,
+            recv_sem=recv,
+            device_id=device,
+            device_id_type=pl.DeviceIdType.MESH,
+        )
+
+    def loop(low, high, body):
+        def step(i, none):
+            body(i)
+            return none
+
+        lax.fori_loop(low, high, step, 0)
+
+    barrier = pltpu.get_barrier_semaphore()
+
+    def greet(k):
+        other = lax.rem(me + k, devices)
+        pl.semaphore_signal(
+            barrier,
+            inc=1,
+            device_id=(other // gy_count, lax.rem(other, gy_count)),
+            device_id_type=pl.DeviceIdType.MESH,
+        )
+
+    loop(1, devices, greet)
+    pl.semaphore_wait(barrier, devices - 1)
+
+    def block(z_at, core_at, gy_at):
+        return (z_at * 2 + core_at) * gy_count + gy_at
+
+    def chip(k):
+        return lax.rem(z + k, chips)
+
+    def plane(k):
+        return lax.rem(gy + k, gy_count)
+
+    def along_line(k):
+        return remote(
+            own_ref, grads_ref.at[me], line_send.at[k], block_recv.at[me],
+            (chip(k) * 2 + core, gy),
+        )
+
+    def in_plane(k, m):
+        at = block(chip(k), core, gy)
+        return remote(
+            grads_ref.at[at], grads_ref.at[at], plane_send.at[k, m], block_recv.at[at],
+            (gx, plane(m)),
+        )
+
+    def own_in_plane(m):
+        return remote(
+            own_ref, grads_ref.at[me], plane_send.at[0, m], block_recv.at[me], (gx, plane(m))
+        )
+
+    def to_core(at):
+        return remote(
+            grads_ref.at[at], grads_ref.at[at], core_send.at[at], block_recv.at[at], sibling
+        )
+
+    own_to_core = remote(own_ref, grads_ref.at[me], core_send.at[me], block_recv.at[me], sibling)
+    pair = remote(part_ref.at[:, 1 - core], pair_in, pair_sems.at[0], pair_sems.at[1], sibling)
+    keep = pltpu.make_async_copy(own_ref, grads_ref.at[me], keep_sem)
+    loop(1, chips, lambda k: along_line(k).start())
+    pair.start()
+    loop(1, gy_count, lambda m: own_in_plane(m).start())
+    own_to_core.start()
+    keep.start()
+
     earlier = one_hot(
         lax.broadcasted_iota(jnp.int32, (bags, bags), 0)
         < lax.broadcasted_iota(jnp.int32, (bags, bags), 1)
@@ -29,34 +115,189 @@
     owner_ids = lax.broadcasted_iota(jnp.int32, (devices, bags), 0)
     slot_ids = lax.broadcasted_iota(jnp.int32, (capacity, bags), 0)
     bag_ids = lax.broadcasted_iota(jnp.int32, (1, bags), 1).astype(f32)
-    for table in range(tables):
-        carry = jnp.zeros((devices, 1), f32)
-        total = jnp.zeros((3 * devices, capacity), f32)
-        for item in range(bag_size):
-            at = table * bag_size + item
-            owner = owner_ref[at : at + 1, :]
-            row = row_ref[at : at + 1, :] + LOW
-            hit = owner == owner_ids
-            member = jnp.where(hit, 1.0, 0.0)
-            before = lax.dot_general(
-                member.astype(jnp.bfloat16),
-                earlier,
-                (((1,), (0,)), ((), ())),
+    bag_size = owner_ref.shape[0] // tables
+
+    def pack(table):
+        def item(i, state):
+            carry, total = state
+            lefts, rights = [], []
+            owners = owner_ref[pl.ds(table * bag_size + i * 8, 8), :]
+            rows = row_ref[pl.ds(table * bag_size + i * 8, 8), :] + LOW
+            highs = (rows // LOW).astype(f32)
+            lows = (rows % LOW).astype(f32)
+            for k in range(8):
+                member = jnp.where(owners[k : k + 1] == owner_ids, 1.0, 0.0)
+                before = lax.dot_general(
+                    member.astype(jnp.bfloat16),
+                    earlier,
+                    (((1,), (0,)), ((), ())),
+                    preferred_element_type=f32,
+                )
+                slot = jnp.sum(member * (before + carry), axis=0, keepdims=True)
+                carry = carry + jnp.sum(member, axis=1, keepdims=True)
+                lefts.append(
+                    jnp.concatenate(
+                        [member * bag_ids, member * highs[k : k + 1], member * lows[k : k + 1]],
+                        axis=0,
+                    ).astype(jnp.bfloat16)
+                )
+                rights.append(one_hot(slot.astype(jnp.int32) == slot_ids))
+            total = total + lax.dot_general(
+                jnp.concatenate(lefts, axis=1),
+                jnp.concatenate(rights, axis=1),
+                (((1,), (1,)), ((), ())),
                 preferred_element_type=f32,
             )
-            slot = jnp.sum(member * (before + carry), axis=0, keepdims=True)
-            carry = carry + jnp.sum(member, axis=1, keepdims=True)
-            high = (row // LOW).astype(f32)
-            low = (row % LOW).astype(f32)
-            left = jnp.concatenate(
-                [member * bag_ids, member * high, member * low], axis=0
-            ).astype(jnp.bfloat16)
-            right = one_hot(slot.astype(jnp.int32) == slot_ids)
-            total = total + lax.dot_general(
-                left, right, (((1,), (1,)), ((), ())), preferred_element_type=f32
-            )
+            return carry, total
+
+        _, total = lax.fori_loop(
+            0,
+            bag_size // 8,
+            item,
+            (jnp.zeros((devices, 1), f32), jnp.zeros((3 * devices, capacity), f32)),
+        )
         code = total[:devices] * BAG_STEP + total[devices : 2 * devices] * LOW + total[2 * devices :]
-        codes_ref[:, table * capacity : (table + 1) * capacity] = code.astype(jnp.int32)
+        lists[:, table * capacity : (table + 1) * capacity] = code.astype(jnp.int32)
+
+    pack(0)
+
+    pair.wait_recv()
+
+    def pair_add(g):
+        pair_sum[g] = part_ref[g, core] + pair_in[g]
+
+    loop(0, gy_count, pair_add)
+
+    def plane_sums(m):
+        return remote(
+            pair_sum.at[plane(m)], plane_in.at[gy], plane_sum_send.at[m], plane_sum_recv.at[gy],
+            (gx, plane(m)),
+        )
+
+    loop(1, gy_count, lambda m: plane_sums(m).start())
+
+    def forward_line(k):
+        at = block(chip(k), core, gy)
+        to_core(at).wait_recv()
+        loop(1, gy_count, lambda m: in_plane(k, m).start())
+        to_core(at).start()
+
+    loop(1, chips, forward_line)
+
+    for table in range(1, tables):
+        pack(table)
+    lines = outgoing.shape[1]
+    for k in range(lines):
+        outgoing[:, k, :] = lists[:, k * 128 : (k + 1) * 128]
+    codes_ref[me] = outgoing[me]
+
+    def code_to(k):
+        other = lax.rem(me + k, devices)
+        return remote(
+            outgoing.at[other], codes_ref.at[me], code_send.at[k], code_recv.at[me],
+            (other // gy_count, lax.rem(other, gy_count)),
+        )
+
+    loop(1, devices, lambda k: code_to(k).start())
+
+    plane_sum[...] = pair_sum[gy]
+
+    def plane_add(m):
+        at = plane(m)
+        remote(
+            plane_in.at[at], plane_in.at[at], plane_sum_send.at[m], plane_sum_recv.at[at], sibling
+        ).wait_recv()
+        plane_sum[...] += plane_in[at]
+
+    loop(1, gy_count, plane_add)
+
+    def line_sums(k):
+        return remote(
+            plane_sum.at[chip(k)], line_in.at[z], line_sum_send.at[k], line_sum_recv.at[z],
+            (chip(k) * 2 + core, gy),
+        )
+
+    loop(1, chips, lambda k: line_sums(k).start())
+
+    def forward_plane(m):
+        def one(k):
+            at = block(chip(k), core, plane(m))
+            to_core(at).wait_recv()
+            to_core(at).start()
+
+        loop(0, chips, one)
+
+    loop(1, gy_count, forward_plane)
+
+    sums_ref[core, z] = plane_sum[z]
+
+    def line_add(k):
+        at = chip(k)
+        remote(
+            line_in.at[at], line_in.at[at], line_sum_send.at[k], line_sum_recv.at[at], sibling
+        ).wait_recv()
+        sums_ref[core, z] += line_in[at]
+
+    loop(1, chips, line_add)
+
+    def back(k):
+        return remote(
+            sums_ref.at[core, z], sums_ref.at[core, z], back_send.at[k], back_recv.at[core, z],
+            (chip(k) * 2 + core, gy),
+        )
+
+    def back_core(k):
+        at = chip(k)
+        return remote(
+            sums_ref.at[core, at], sums_ref.at[core, at], back_core_send.at[k],
+            back_recv.at[core, at], sibling,
+        )
+
+    def back_arrived(core_at, at):
+        return remote(
+            sums_ref.at[core_at, at], sums_ref.at[core_at, at], back_core_send.at[0],
+            back_recv.at[core_at, at], sibling,
+        )
+
+    loop(1, chips, lambda k: back(k).start())
+    back_core(0).start()
+
+    def forward_back(k):
+        back_arrived(core, chip(k)).wait_recv()
+        back_core(k).start()
+
+    loop(1, chips, forward_back)
+
+    def code_arrived(k):
+        at = lax.rem(me + k, devices)
+        remote(
+            codes_ref.at[at], codes_ref.at[at], code_send.at[k], code_recv.at[at], sibling
+        ).wait_recv()
+
+    loop(1, devices, code_arrived)
+    loop(0, chips, lambda k: back_arrived(1 - core, k).wait_recv())
+
+    def core_arrived(k):
+        loop(0, gy_count, lambda g: to_core(block(k, 1 - core, g)).wait_recv())
+
+    loop(0, chips, core_arrived)
+    keep.wait()
+    pair.wait_send()
+    own_to_core.wait_send()
+    loop(1, chips, lambda k: along_line(k).wait_send())
+    loop(1, gy_count, lambda m: own_in_plane(m).wait_send())
+    loop(1, chips, lambda k: loop(1, gy_count, lambda m: in_plane(k, m).wait_send()))
+    loop(1, chips, lambda k: to_core(block(chip(k), core, gy)).wait_send())
+    loop(
+        1,
+        gy_count,
+        lambda m: loop(0, chips, lambda k: to_core(block(chip(k), core, plane(m))).wait_send()),
+    )
+    loop(1, gy_count, lambda m: plane_sums(m).wait_send())
+    loop(1, chips, lambda k: line_sums(k).wait_send())
+    loop(1, chips, lambda k: back(k).wait_send())
+    loop(0, chips, lambda k: back_core(k).wait_send())
+    loop(1, devices, lambda k: code_to(k).wait_send())
 
 
 def add_kernel(capacity, tables, bags, width, sub, codes_ref, grads_ref, out_ref):
@@ -106,16 +347,54 @@
                 ]
 
 
-def pack_codes(owner_lists, row_lists, devices, capacity, tables):
+def exchange(owner_lists, row_lists, own, part, gx_count, gy_count, capacity, tables):
+    devices = gx_count * gy_count
+    chips = gx_count // 2
+    bags, both = own.shape
+    q, columns = part.shape[3:]
+    lines = tables * capacity // 128
+    f32 = jnp.float32
+    vmem = pl.BlockSpec(memory_space=pltpu.VMEM)
+    dma = pltpu.SemaphoreType.DMA
     return pl.pallas_call(
-        functools.partial(pack_kernel, devices, capacity, tables),
-        out_shape=jax.ShapeDtypeStruct((devices, tables * capacity), jnp.int32),
-        in_specs=[pl.BlockSpec(memory_space=pltpu.VMEM)] * 2,
-        out_specs=pl.BlockSpec(memory_space=pltpu.VMEM),
-        compiler_params=pltpu.CompilerParams(vmem_limit_bytes=32 * 2**20),
-        cost_estimate=pl.CostEstimate(flops=2 * 10**9, bytes_accessed=10**6, transcendentals=0),
-        name="pack",
-    )(owner_lists, row_lists)
+        functools.partial(exchange_kernel, gx_count, gy_count, capacity, tables),
+        out_shape=(
+            jax.ShapeDtypeStruct((devices, bags, both), jnp.bfloat16),
+            jax.ShapeDtypeStruct((devices, lines, 128), jnp.int32),
+            jax.ShapeDtypeStruct((2, chips, q, columns), f32),
+        ),
+        in_specs=[vmem] * 4,
+        out_specs=(pl.BlockSpec(memory_space=pl.ANY), vmem, vmem),
+        scratch_shapes=[
+            pltpu.VMEM((devices, tables * capacity), jnp.int32),
+            pltpu.VMEM((devices, lines, 128), jnp.int32),
+            pltpu.VMEM((gy_count, chips, q, columns), f32),
+            pltpu.VMEM((gy_count, chips, q, columns), f32),
+            pltpu.VMEM((gy_count, chips, q, columns), f32),
+            pltpu.VMEM((chips, q, columns), f32),
+            pltpu.VMEM((chips, q, columns), f32),
+            dma(()),
+            dma((chips,)),
+            dma((chips, gy_count)),
+            dma((devices,)),
+            dma((devices,)),
+            dma((devices,)),
+            dma((devices,)),
+            dma((2,)),
+            dma((gy_count,)),
+            dma((gy_count,)),
+            dma((chips,)),
+            dma((chips,)),
+            dma((chips,)),
+            dma((chips,)),
+            dma((2, chips)),
+        ],
+        compiler_params=pltpu.CompilerParams(
+            vmem_limit_bytes=48 * 2**20, collective_id=0, has_side_effects=True
+        ),
+        cost_estimate=pl.CostEstimate(flops=2 * 10**9, bytes_accessed=10**7, transcendentals=0),
+        name="exchange",
+    )(owner_lists, row_lists, own, part)
 
 
 def add_rows(codes, grads, capacity, tables, bags, width, local_rows):
@@ -144,33 +423,54 @@
     tables = pooled.shape[1]
     width = pooled.shape[2]
     bag_size = lookup_owner.shape[2]
-    devices = lax.axis_size("gx") * lax.axis_size("gy")
+    gx_count, gy_count = lax.axis_size("gx"), lax.axis_size("gy")
+    devices = gx_count * gy_count
     capacity = max(2, 2 * bags * bag_size // devices)
+    f32 = jnp.float32
     top_grad = jnp.where(top_pre > 0, top_cotangent, jnp.zeros_like(top_cotangent))
     feature_grad = lax.dot_general(
-        top_grad, top_weight, (((1,), (1,)), ((), ())), preferred_element_type=jnp.float32
+        top_grad, top_weight, (((1,), (1,)), ((), ())), preferred_element_type=f32
     ).astype(jnp.bfloat16)
-    grads = lax.all_gather(feature_grad[:, width:], AXES, axis=0, tiled=True)
     owner_lists = lookup_owner.reshape(bags, tables * bag_size).T
     row_lists = lookup_row.reshape(bags, tables * bag_size).T
-    codes = pack_codes(owner_lists, row_lists, devices, capacity, tables)
-    codes = lax.all_to_all(codes, AXES, split_axis=0, concat_axis=0, tiled=True)
     bottom_out = jnp.maximum(bottom_pre, jnp.zeros_like(bottom_pre))
     feature = jnp.concatenate([bottom_out, pooled.reshape(bags, tables * width)], axis=1)
     top_weight_part = lax.dot_general(
-        feature, top_grad, (((0,), (0,)), ((), ())), preferred_element_type=jnp.float32
-    )
-    top_bias_part = jnp.sum(top_grad.astype(jnp.float32), axis=0)
+        feature, top_grad, (((0,), (0,)), ((), ())), preferred_element_type=f32
+    )
+    top_bias_part = jnp.sum(top_grad.astype(f32), axis=0)
     bottom_grad = jnp.where(bottom_pre > 0, feature_grad[:, :width], jnp.zeros_like(bottom_pre))
     bottom_weight_part = lax.dot_general(
-        bottom_in, bottom_grad, (((0,), (0,)), ((), ())), preferred_element_type=jnp.float32
-    )
-    shares = (
-        lax.psum_scatter(top_weight_part, "gy", scatter_dimension=0, tiled=True),
-        lax.psum_scatter(top_bias_part, "gy", scatter_dimension=0, tiled=True),
-        lax.psum_scatter(bottom_weight_part, "gy", scatter_dimension=0, tiled=True),
-    )
-    top_weight_grad, top_bias_grad, bottom_weight_grad = lax.psum(shares, "gx")
+        bottom_in, bottom_grad, (((0,), (0,)), ((), ())), preferred_element_type=f32
+    )
+    columns = top_weight_part.shape[1]
+    top_rows = top_weight_part.shape[0] // gy_count
+    bottom_rows = bottom_weight_part.shape[0] // gy_count
+    bias_share = columns // gy_count
+    bottom_lines = bottom_rows * width // columns
+    used = top_rows + bottom_lines + 1
+    q = -(-used // (gx_count * 8)) * 8
+    bias_lines = jnp.pad(
+        top_bias_part.reshape(gy_count, 1, bias_share),
+        ((0, 0), (0, gx_count * q - used), (0, columns - bias_share)),
+    )
+    part = jnp.concatenate(
+        [
+            top_weight_part.reshape(gy_count, top_rows, columns),
+            bottom_weight_part.reshape(gy_count, bottom_lines, columns),
+            bias_lines,
+        ],
+        axis=1,
+    ).reshape(gy_count, 2, gx_count // 2, q, columns)
+    grads, codes, sums = exchange(
+        owner_lists, row_lists, feature_grad[:, width:], part, gx_count, gy_count, capacity, tables
+    )
+    sums = sums.reshape(gx_count * q, columns)
+    top_weight_grad = sums[:top_rows]
+    bottom_weight_grad = sums[top_rows : top_rows + bottom_lines].reshape(bottom_rows, width)
+    top_bias_grad = sums[top_rows + bottom_lines, :bias_share]
+    codes = codes.reshape(devices, tables * capacity)
+    grads = grads.reshape(devices * bags, tables * width)
     table_grad = add_rows(codes, grads, capacity, tables, bags, width, ROWS_DEV)
     return (table_grad, top_weight_grad, top_bias_grad, bottom_weight_grad)
 

time: 146 us -> 92.4 us (0.63)
  blocking collectives: 39.3 us -> 0 us
  Pallas kernels: 43.8 us -> 80.4 us
  waiting for transfers between devices: 25.7 us -> 0 us
  between operations: 16 us -> 0.79 us
  starting transfers between devices: 7.46 us -> 0 us
  local copies, waits for them, and re-layouts: 9.65 us -> 5.84 us
  other arithmetic: 0.21 us -> 2.68 us
    pallas_call x1, Pallas kernels: 15.6 us -> 52.2 us  [exchange(): pl.pallas_call(functools.partial(exchange_kernel, gx_count, gy_count, cap...]
    psum x1 -> x0, blocking collectives: 29.1 us -> none  [shards(): top_weight_grad, top_bias_grad, bottom_weight_grad = lax.psum(shares, 'gx')]
    psum x1 -> x0, waiting for transfers between devices: 24.1 us -> none  [shards(): top_weight_grad, top_bias_grad, bottom_weight_grad = lax.psum(shares, 'gx')]
    unnamed x1 -> x0, blocking collectives: 10.1 us -> none
    all_to_all x1 -> x0, starting transfers between devices: 7.29 us -> none  [shards(): codes = lax.all_to_all(codes, AXES, split_axis=0, concat_axis=0, tiled=True)]
    unnamed x28 -> x17, local copies, waits for them, and re-layouts: 8.2 us -> 3.71 us
    all_gather x1 -> x0, waiting for transfers between devices: 1.54 us -> none  [shards(): grads = lax.all_gather(feature_grad[:, width:], AXES, axis=0, tiled=True)]
  transfers between devices with their start and end apart: 5 -> 0, of which waited for: 2 -> 0; matrix products, arithmetic and copies ran while one was open for 4% -> 0% of each run, Pallas kernels for 30% -> 0%
where the time goes in v2:
time: 92.4 us; the launch traced here: 91.9 us
  Pallas kernels  80.4 us (87%)
  local copies, waits for them, and re-layouts  5.84 us (6%)
  other arithmetic  2.68 us (3%)
  matrix products  2.25 us (2%)
    pallas_call x1, Pallas kernels, exchange(): pl.pallas_call(functools.partial(exchange_kernel, gx_count, gy_count, cap...  52.2 us
    pallas_call x1, Pallas kernels, add_rows(): pl.pallas_call(functools.partial(add_kernel, capacity, tables, bags, widt...  28.2 us
    unnamed x17, local copies, waits for them, and re-layouts  3.71 us

profile of v2, /device:TPU:0, one launch (start us, length us, event | category | flops | bytes accessed | tf_op | source)
XLA Modules:
  0.0 91.9 jit_solution(1685511012627769927)
XLA Ops:
  0.6 0.0 copy-start
  0.6 0.0 copy-start.6
  0.7 0.0 copy-start.7
  0.7 1.5 %convert_reduce_fusion = f32[1024]{0:T(1024)S(1)} fusion(bf16[256,1024]{1,0:T(8,128)(2,1)} %param.12, bf16[256,1024]{1,0:T(8,128)(2,1)} %param.11), kind=kLoop, calls=%fused_computation.4 | loop fusion | flops 1047552 | bytes 1052672 | tf_op jit(solution)/shard_map/reduce_sum | solution.py:441
  2.1 0.0 copy-start.4
  2.2 0.0 copy-start.5
  2.2 0.9 %broadcast_maximum_fusion = bf16[256,128]{1,0:T(8,128)(2,1)S(1)} fusion(bf16[256,128]{1,0:T(8,128)(2,1)} %param.9), kind=kLoop, calls=%fused_computation.14 | loop fusion | flops 32768 | bytes 131072 | tf_op jit(solution)/shard_map/max | solution.py:436
  3.1 0.9 %copy.15 = bf16[32,8,2,128]{3,1,2,0:T(8,128)(2,1)S(1)} copy(bf16[32,8,2,128]{3,2,1,0:T(2,128)(2,1)} %bitcast.29) | data formatting | bytes 262144
  4.0 0.0 copy-done
  4.0 1.7 %convolution_convert_fusion = bf16[256,384]{1,0:T(8,128)(2,1)S(1)} fusion(bf16[384,1024]{1,0:T(8,128)(2,1)S(1)} %copy-done, bf16[256,1024]{1,0:T(8,128)(2,1)} %param.12, bf16[256,1024]{1,0:T(8,128)(2,1)} %param.11), kind=kOutput, calls=%fused_computation.2 | convolution fusion | flops 201949184 | bytes 2031616 | tf_op jit(solution)/shard_map/dot_general | solution.py:431
  5.7 0.0 copy-done.6
  5.7 0.0 copy-done.7
  5.7 0.2 convolution_bitcast_fusion
  5.9 0.1 copy.12
  6.1 0.0 copy-done.4
  6.1 0.0 copy-done.5
  6.1 0.4 fusion
  6.5 0.0 copy-start.1
  6.5 0.0 copy-start.2
  6.5 0.3 select_maximum_fusion
  6.8 0.5 copy-done.1
  7.3 0.0 copy-done.2
  7.4 52.2 %exchange.1 = (bf16[32,256,256]{2,1,0:T(8,128)(2,1)}, s32[32,8,128]{2,1,0:T(8,128)S(1)}, f32[2,4,16,1024]{3,2,1,0:T(8,128)S(1)}) custom-call(s32[64,256]{1,0:T(8,128)S(1)} %bitcast.24, s32[64,256]{1,0:T(8,128)S(1)} %bitcast.25, bf16[256,256]{1,0:T(8,128)(2,1)S(1)} %slice.20.own_ref, f32[4,2,4,16,1024]{4,3,2,1,0:T(8,128)S(1)} %bitcast.20), custom_call_target="tpu_custom_call" | custom-call | flops 2000000000 | bytes 10000000 | tf_op jit(solution)/shard_map/exchange/pallas_call | solution.py:359
  59.6 0.0 copy-start.3
  59.6 2.2 %copy-done.3 = bf16[32,256,256]{2,1,0:T(8,128)(2,1)S(1)} copy-done((bf16[32,256,256]{2,1,0:T(8,128)(2,1)S(1)}, bf16[32,256,256]{2,1,0:T(8,128)(2,1)}, u32[]{:S(2)}) %copy-start.3) | copy-done | bytes 4194328
  61.8 28.2 %add_rows.1 = f32[2,2048,128]{2,1,0:T(8,128)} custom-call(s32[4,8,1024]{2,1,0:T(8,128)S(1)} %reshape_reshape.3.codes_ref, bf16[8192,256]{1,0:T(8,128)(2,1)S(1)} %bitcast.26), custom_call_target="tpu_custom_call" | custom-call | flops 40000000000 | bytes 8000000 | tf_op jit(solution)/shard_map/add_rows/pallas_call | solution.py:404
  90.0 0.6 slice.23
  90.5 0.8 slice.22
  91.3 0.6 reshape.47
  (4 shorter events, 0.1 us)
Async XLA Ops:
  0.6 3.4 %copy-start = (bf16[384,1024]{1,0:T(8,128)(2,1)S(1)}, bf16[384,1024]{1,0:T(8,128)(2,1)}, u32[]{:S(2)}) copy-start(bf16[384,1024]{1,0:T(8,128)(2,1)} %param.13) | copy-start | bytes 2359300
  0.6 5.1 %copy-start.6 = (bf16[256,128]{1,0:T(8,128)(2,1)S(1)}, bf16[256,128]{1,0:T(8,128)(2,1)}, u32[]{:S(2)}) copy-start(bf16[256,128]{1,0:T(8,128)(2,1)} %param.9) | copy-start | bytes 196612
  0.7 5.1 %copy-start.7 = (bf16[256,256]{1,0:T(8,128)(2,1)S(1)}, bf16[256,256]{1,0:T(8,128)(2,1)}, u32[]{:S(2)}) copy-start(bf16[256,256]{1,0:T(8,128)(2,1)} %param.8) | copy-start | bytes 393220
  2.1 3.9 %copy-start.4 = (bf16[256,1024]{1,0:T(8,128)(2,1)S(1)}, bf16[256,1024]{1,0:T(8,128)(2,1)}, u32[]{:S(2)}) copy-start(bf16[256,1024]{1,0:T(8,128)(2,1)} %param.12) | copy-start | bytes 1572868
  2.2 3.9 %copy-start.5 = (bf16[256,1024]{1,0:T(8,128)(2,1)S(1)}, bf16[256,1024]{1,0:T(8,128)(2,1)}, u32[]{:S(2)}) copy-start(bf16[256,1024]{1,0:T(8,128)(2,1)} %param.11) | copy-start | bytes 1572868
  6.5 0.8 copy-start.1
  6.5 0.9 copy-start.2
  59.6 2.2 %copy-start.3 = (bf16[32,256,256]{2,1,0:T(8,128)(2,1)S(1)}, bf16[32,256,256]{2,1,0:T(8,128)(2,1)}, u32[]{:S(2)}) copy-start(bf16[32,256,256]{2,1,0:T(8,128)(2,1)} %get-tuple-element.8) | copy-start | bytes 12582916

commit v3 on v2

--- a/solution.py
+++ b/solution.py
@@ -14,15 +14,21 @@
 AXES = ("gx", "gy")
 
 
-def one_hot(condition):
-    return jnp.where(condition, 1.0, 0.0).astype(jnp.bfloat16)
+def one_hot(left, right):
+    one = jnp.ones((), jnp.bfloat16)
+    return jnp.where(left == right, one, jnp.zeros((), jnp.bfloat16))
+
+
+def count(shape, axis, less=0):
+    numbers = lax.broadcasted_iota(jnp.int32, shape, axis) - less
+    return numbers.astype(jnp.float32).astype(jnp.bfloat16)
 
 
 def exchange_kernel(
     gx_count, gy_count, capacity, tables,
     owner_ref, row_ref, own_ref, part_ref,
-    grads_ref, codes_ref, sums_ref,
-    lists, outgoing, pair_in, pair_sum, plane_in, plane_sum, line_in,
+    table_ref, sums_ref,
+    grads_ref, codes_ref, lists, outgoing, pair_in, pair_sum, plane_in, plane_sum, line_in,
     keep_sem, line_send, plane_send, core_send, block_recv, code_send, code_recv,
     pair_sems, plane_sum_send, plane_sum_recv, line_sum_send, line_sum_recv,
     back_send, back_core_send, back_recv,
@@ -108,40 +114,48 @@
     own_to_core.start()
     keep.start()
 
-    earlier = one_hot(
+    half = capacity // 2
+    bf16 = jnp.bfloat16
+    earlier = jnp.where(
         lax.broadcasted_iota(jnp.int32, (bags, bags), 0)
-        < lax.broadcasted_iota(jnp.int32, (bags, bags), 1)
-    )
-    owner_ids = lax.broadcasted_iota(jnp.int32, (devices, bags), 0)
-    slot_ids = lax.broadcasted_iota(jnp.int32, (capacity, bags), 0)
-    bag_ids = lax.broadcasted_iota(jnp.int32, (1, bags), 1).astype(f32)
+        < lax.broadcasted_iota(jnp.int32, (bags, bags), 1),
+        1.0,
+        0.0,
+    ).astype(bf16)
+    owner_ids = count((devices, bags), 0)
+    slot_ids = count((capacity, bags), 0, half)
+    bag_line = count((1, bags), 1)
+    nothing = jnp.zeros((), bf16)
     bag_size = owner_ref.shape[0] // tables
 
     def pack(table):
         def item(i, state):
             carry, total = state
             lefts, rights = [], []
-            owners = owner_ref[pl.ds(table * bag_size + i * 8, 8), :]
+            owners = owner_ref[pl.ds(table * bag_size + i * 8, 8), :].astype(f32)
             rows = row_ref[pl.ds(table * bag_size + i * 8, 8), :] + LOW
             highs = (rows // LOW).astype(f32)
             lows = (rows % LOW).astype(f32)
             for k in range(8):
-                member = jnp.where(owners[k : k + 1] == owner_ids, 1.0, 0.0)
+                hit = owners[k : k + 1].astype(bf16) == owner_ids
+                member = jnp.where(hit, jnp.ones((), bf16), nothing)
                 before = lax.dot_general(
-                    member.astype(jnp.bfloat16),
-                    earlier,
-                    (((1,), (0,)), ((), ())),
-                    preferred_element_type=f32,
+                    member, earlier, (((1,), (0,)), ((), ())), preferred_element_type=f32
                 )
-                slot = jnp.sum(member * (before + carry), axis=0, keepdims=True)
-                carry = carry + jnp.sum(member, axis=1, keepdims=True)
+                wide = member.astype(f32)
+                slot = jnp.sum(wide * (before + carry), axis=0, keepdims=True)
+                carry = carry + jnp.sum(wide, axis=1, keepdims=True)
                 lefts.append(
                     jnp.concatenate(
-                        [member * bag_ids, member * highs[k : k + 1], member * lows[k : k + 1]],
+                        [
+                            member * bag_line,
+                            member * highs[k : k + 1].astype(bf16),
+                            member * lows[k : k + 1].astype(bf16),
+                        ],
                         axis=0,
-                    ).astype(jnp.bfloat16)
+                    )
                 )
-                rights.append(one_hot(slot.astype(jnp.int32) == slot_ids))
+                rights.append(one_hot((slot - half).astype(bf16), slot_ids))
             total = total + lax.dot_general(
                 jnp.concatenate(lefts, axis=1),
                 jnp.concatenate(rights, axis=1),
@@ -200,6 +214,73 @@
 
     loop(1, devices, lambda k: code_to(k).start())
 
+    def code_arrived(at):
+        remote(
+            codes_ref.at[at], codes_ref.at[at], code_send.at[0], code_recv.at[at], sibling
+        ).wait_recv()
+
+    table_ref[...] = jnp.zeros_like(table_ref)
+    parts = table_ref.shape[1] // ROW_BLOCK
+    width = table_ref.shape[2]
+    piece = min(capacity, 128)
+    pieces = capacity // piece
+    bag_ids = count((piece, bags), 1)
+    row_ids = count((ROW_BLOCK, capacity), 0, ROW_BLOCK // 2)
+
+    def add_unit(core_at, gy_at):
+        lefts = [[] for _ in range(tables)]
+        rights = [[] for _ in range(tables)]
+        for k in range(chips):
+            at = block(chip(k), core_at, gy_at)
+            codes = codes_ref[at]
+            if lines % 8:
+                codes = jnp.broadcast_to(codes[:1], (8, 128))
+            row_form = codes % BAG_STEP - LOW
+            row_low = ((row_form & (ROW_BLOCK - 1)) - ROW_BLOCK // 2).astype(f32)
+            row_part = jnp.transpose((row_form >> (ROW_BLOCK.bit_length() - 1)).astype(f32))
+            bag_form = jnp.transpose((codes // BAG_STEP).astype(f32))
+            for table in range(tables):
+                low_pieces, picked_pieces, part_pieces = [], [], []
+                for p in range(pieces):
+                    spot = table * capacity + p * piece
+                    line, lane = spot // 128, spot % 128
+                    low_pieces.append(row_low[line : line + 1, lane : lane + piece])
+                    bag = bag_form[lane : lane + piece, line : line + 1]
+                    picked_pieces.append(
+                        one_hot(jnp.broadcast_to(bag, (piece, bags)).astype(bf16), bag_ids)
+                    )
+                    part = row_part[lane : lane + piece, line : line + 1]
+                    part_pieces.append(jnp.broadcast_to(part, (piece, width)).astype(bf16))
+                low = jnp.concatenate(low_pieces, axis=1).astype(bf16)
+                lefts[table].append(one_hot(low, row_ids))
+                picked = lax.dot_general(
+                    jnp.concatenate(picked_pieces, axis=0),
+                    grads_ref[at, :, table * width : (table + 1) * width],
+                    (((1,), (0,)), ((), ())),
+                    preferred_element_type=f32,
+                ).astype(bf16)
+                part = jnp.concatenate(part_pieces, axis=0)
+                rights[table].append(
+                    jnp.concatenate(
+                        [
+                            jnp.where(part == jnp.full((), p, bf16), picked, nothing)
+                            for p in range(parts)
+                        ],
+                        axis=1,
+                    )
+                )
+        for table in range(tables):
+            result = lax.dot_general(
+                jnp.concatenate(lefts[table], axis=1),
+                jnp.concatenate(rights[table], axis=0),
+                (((1,), (0,)), ((), ())),
+                preferred_element_type=f32,
+            )
+            for p in range(parts):
+                table_ref[table, p * ROW_BLOCK : (p + 1) * ROW_BLOCK, :] += result[
+                    :, p * width : (p + 1) * width
+                ]
+
     plane_sum[...] = pair_sum[gy]
 
     def plane_add(m):
@@ -219,6 +300,8 @@
 
     loop(1, chips, lambda k: line_sums(k).start())
 
+    keep.wait()
+
     def forward_plane(m):
         def one(k):
             at = block(chip(k), core, plane(m))
@@ -227,7 +310,20 @@
 
         loop(0, chips, one)
 
-    loop(1, gy_count, forward_plane)
+    loop(1, chips, lambda k: code_arrived(block(chip(k), core, gy)))
+
+    def own_core_unit(m):
+        @pl.when(m < gy_count - 1)
+        def _():
+            forward_plane(m + 1)
+
+        @pl.when(m > 0)
+        def _():
+            loop(0, chips, lambda k: code_arrived(block(chip(k), core, plane(m))))
+
+        add_unit(core, plane(m))
+
+    loop(0, gy_count, own_core_unit)
 
     sums_ref[core, z] = plane_sum[z]
 
@@ -262,26 +358,26 @@
     loop(1, chips, lambda k: back(k).start())
     back_core(0).start()
 
+    def other_core_unit(m):
+        def arrive(k):
+            at = block(chip(k), 1 - core, plane(m))
+            code_arrived(at)
+            to_core(at).wait_recv()
+
+        loop(0, chips, arrive)
+        add_unit(1 - core, plane(m))
+
+    loop(0, gy_count - 1, other_core_unit)
+
     def forward_back(k):
         back_arrived(core, chip(k)).wait_recv()
         back_core(k).start()
 
     loop(1, chips, forward_back)
-
-    def code_arrived(k):
-        at = lax.rem(me + k, devices)
-        remote(
-            codes_ref.at[at], codes_ref.at[at], code_send.at[k], code_recv.at[at], sibling
-        ).wait_recv()
-
-    loop(1, devices, code_arrived)
+    other_core_unit(gy_count - 1)
+
     loop(0, chips, lambda k: back_arrived(1 - core, k).wait_recv())
 
-    def core_arrived(k):
-        loop(0, gy_count, lambda g: to_core(block(k, 1 - core, g)).wait_recv())
-
-    loop(0, chips, core_arrived)
-    keep.wait()
     pair.wait_send()
     own_to_core.wait_send()
     loop(1, chips, lambda k: along_line(k).wait_send())
@@ -300,53 +396,6 @@
     loop(1, devices, lambda k: code_to(k).wait_send())
 
 
-def add_kernel(capacity, tables, bags, width, sub, codes_ref, grads_ref, out_ref):
-    f32 = jnp.float32
-    group = codes_ref.shape[1]
-    local_rows = out_ref.shape[1]
-    parts = local_rows // ROW_BLOCK
-
-    @pl.when(pl.program_id(0) == 0)
-    def _():
-        out_ref[...] = jnp.zeros_like(out_ref)
-
-    codes = codes_ref[0]
-    columns = jnp.transpose(codes)
-    bag_ids = lax.broadcasted_iota(jnp.int32, (capacity, bags), 1)
-    row_ids = lax.broadcasted_iota(jnp.int32, (ROW_BLOCK, capacity), 0)
-    for table in range(tables):
-        for first in range(0, group, sub):
-            lefts, rights = [], []
-            for source in range(first, first + sub):
-                spot = slice(table * capacity, (table + 1) * capacity)
-                line = codes[source : source + 1, spot] % BAG_STEP - LOW
-                lefts.append(one_hot((line & (ROW_BLOCK - 1)) == row_ids))
-                column = columns[spot, source : source + 1]
-                picked = lax.dot_general(
-                    one_hot((column // BAG_STEP) == bag_ids),
-                    grads_ref[source * bags : (source + 1) * bags, table * width : (table + 1) * width],
-                    (((1,), (0,)), ((), ())),
-                    preferred_element_type=f32,
-                )
-                part = jnp.broadcast_to((column % BAG_STEP - LOW) // ROW_BLOCK, picked.shape)
-                rights.append(
-                    jnp.concatenate(
-                        [jnp.where(part == p, picked, 0.0).astype(jnp.bfloat16) for p in range(parts)],
-                        axis=1,
-                    )
-                )
-            result = lax.dot_general(
-                jnp.concatenate(lefts, axis=1),
-                jnp.concatenate(rights, axis=0),
-                (((1,), (0,)), ((), ())),
-                preferred_element_type=f32,
-            )
-            for p in range(parts):
-                out_ref[table, p * ROW_BLOCK : (p + 1) * ROW_BLOCK, :] += result[
-                    :, p * width : (p + 1) * width
-                ]
-
-
 def exchange(owner_lists, row_lists, own, part, gx_count, gy_count, capacity, tables):
     devices = gx_count * gy_count
     chips = gx_count // 2
@@ -359,13 +408,14 @@
     return pl.pallas_call(
         functools.partial(exchange_kernel, gx_count, gy_count, capacity, tables),
         out_shape=(
-            jax.ShapeDtypeStruct((devices, bags, both), jnp.bfloat16),
-            jax.ShapeDtypeStruct((devices, lines, 128), jnp.int32),
+            jax.ShapeDtypeStruct((tables, ROWS_DEV, both // tables), f32),
             jax.ShapeDtypeStruct((2, chips, q, columns), f32),
         ),
         in_specs=[vmem] * 4,
-        out_specs=(pl.BlockSpec(memory_space=pl.ANY), vmem, vmem),
+        out_specs=(vmem, vmem),
         scratch_shapes=[
+            pltpu.VMEM((devices, bags, both), jnp.bfloat16),
+            pltpu.VMEM((devices, lines, 128), jnp.int32),
             pltpu.VMEM((devices, tables * capacity), jnp.int32),
             pltpu.VMEM((devices, lines, 128), jnp.int32),
             pltpu.VMEM((gy_count, chips, q, columns), f32),
@@ -390,30 +440,11 @@
             dma((2, chips)),
         ],
         compiler_params=pltpu.CompilerParams(
-            vmem_limit_bytes=48 * 2**20, collective_id=0, has_side_effects=True
+            vmem_limit_bytes=60 * 2**20, collective_id=0, has_side_effects=True
         ),
-        cost_estimate=pl.CostEstimate(flops=2 * 10**9, bytes_accessed=10**7, transcendentals=0),
+        cost_estimate=pl.CostEstimate(flops=40 * 10**9, bytes_accessed=10**7, transcendentals=0),
         name="exchange",
     )(owner_lists, row_lists, own, part)
-
-
-def add_rows(codes, grads, capacity, tables, bags, width, local_rows):
-    sources = codes.shape[0]
-    group = 8
-    steps = sources // group
-    return pl.pallas_call(
-        functools.partial(add_kernel, capacity, tables, bags, width, 4),
-        grid=(steps,),
-        out_shape=jax.ShapeDtypeStruct((tables, local_rows, width), jnp.float32),
-        in_specs=[
-            pl.BlockSpec((1, group, tables * capacity), lambda i: (i, 0, 0)),
-            pl.BlockSpec((group * bags, tables * width), lambda i: (i, 0)),
-        ],
-        out_specs=pl.BlockSpec((tables, local_rows, width), lambda i: (0, 0, 0)),
-        compiler_params=pltpu.CompilerParams(vmem_limit_bytes=48 * 2**20),
-        cost_estimate=pl.CostEstimate(flops=40 * 10**9, bytes_accessed=8 * 10**6, transcendentals=0),
-        name="add_rows",
-    )(codes.reshape(steps, group, tables * capacity), grads)
 
 
 def shards(
@@ -462,16 +493,13 @@
         ],
         axis=1,
     ).reshape(gy_count, 2, gx_count // 2, q, columns)
-    grads, codes, sums = exchange(
+    table_grad, sums = exchange(
         owner_lists, row_lists, feature_grad[:, width:], part, gx_count, gy_count, capacity, tables
     )
     sums = sums.reshape(gx_count * q, columns)
     top_weight_grad = sums[:top_rows]
     bottom_weight_grad = sums[top_rows : top_rows + bottom_lines].reshape(bottom_rows, width)
     top_bias_grad = sums[top_rows + bottom_lines, :bias_share]
-    codes = codes.reshape(devices, tables * capacity)
-    grads = grads.reshape(devices * bags, tables * width)
-    table_grad = add_rows(codes, grads, capacity, tables, bags, width, ROWS_DEV)
     return (table_grad, top_weight_grad, top_bias_grad, bottom_weight_grad)
 
 

time: 92.4 us -> 93.4 us (1.011)
  Pallas kernels: 80.4 us -> 76.8 us
  local copies, waits for them, and re-layouts: 5.84 us -> 9.2 us
  other arithmetic: 2.68 us -> 4.05 us
    pallas_call x1 -> x0, Pallas kernels: 28.2 us -> none  [add_rows(): pl.pallas_call(functools.partial(add_kernel, capacity, tables, bags, widt...]
    pallas_call x1, Pallas kernels: 52.2 us -> 76.8 us  [exchange(): pl.pallas_call(functools.partial(exchange_kernel, gx_count, gy_count, cap...]
    concatenate x1, other arithmetic: 0.28 us -> 1.65 us  [shards(): jnp.concatenate([top_weight_part.reshape(gy_count, top_rows, columns), bo...]
    slice x1, local copies, waits for them, and re-layouts: 0.77 us -> 1.77 us  [shards(): top_weight_grad = sums[:top_rows]]
    unnamed x17 -> x12, local copies, waits for them, and re-layouts: 3.71 us -> 4 us
where the time goes in v3:
time: 93.4 us; the launch traced here: 93 us
  Pallas kernels  76.8 us (82%)
  local copies, waits for them, and re-layouts  9.2 us (10%)
  other arithmetic  4.05 us (4%)
  matrix products  2.25 us (2%)
    pallas_call x1, Pallas kernels, exchange(): pl.pallas_call(functools.partial(exchange_kernel, gx_count, gy_count, cap...  76.8 us
    unnamed x12, local copies, waits for them, and re-layouts  4 us

profile of v3, /device:TPU:0, one launch (start us, length us, event | category | flops | bytes accessed | tf_op | source)
XLA Modules:
  0.0 93.0 jit_solution(6860285331386194057)
XLA Ops:
  0.6 0.0 copy-start
  0.6 0.0 copy-start.3
  0.7 0.0 copy-start.4
  0.7 1.5 %convert_reduce_fusion = f32[1024]{0:T(1024)S(1)} fusion(bf16[256,1024]{1,0:T(8,128)(2,1)} %param.12, bf16[256,1024]{1,0:T(8,128)(2,1)} %param.11), kind=kLoop, calls=%fused_computation.4 | loop fusion | flops 1047552 | bytes 1052672 | tf_op jit(solution)/shard_map/reduce_sum | solution.py:472
  2.1 0.0 copy-start.1
  2.2 0.0 copy-start.2
  2.2 0.9 %broadcast_maximum_fusion = bf16[256,128]{1,0:T(8,128)(2,1)S(1)} fusion(bf16[256,128]{1,0:T(8,128)(2,1)} %param.9), kind=kLoop, calls=%fused_computation.14 | loop fusion | flops 32768 | bytes 131072 | tf_op jit(solution)/shard_map/max | solution.py:467
  3.1 0.9 copy.15
  4.0 0.0 copy-done
  4.0 1.7 %convolution_convert_fusion = bf16[256,384]{1,0:T(8,128)(2,1)S(1)} fusion(bf16[384,1024]{1,0:T(8,128)(2,1)S(1)} %copy-done, bf16[256,1024]{1,0:T(8,128)(2,1)} %param.12, bf16[256,1024]{1,0:T(8,128)(2,1)} %param.11), kind=kOutput, calls=%fused_computation.2 | convolution fusion | flops 201949184 | bytes 2031616 | tf_op jit(solution)/shard_map/dot_general | solution.py:462
  5.7 0.0 copy-done.3
  5.7 0.0 copy-done.4
  5.7 0.2 convolution_bitcast_fusion
  5.9 0.7 slice.20.own_ref
  6.6 0.1 copy.12
  6.7 0.0 copy-done.1
  6.7 0.0 copy-done.2
  6.7 0.4 fusion
  7.1 1.6 %select_maximum_fusion = f32[4,128,1024]{2,1,0:T(8,128)} fusion(f32[4,1,256]{2,1,0:T(1,128)S(1)} %bitcast.26, f32[4,8,1024]{2,1,0:T(8,128)S(1)} %reshape.39, f32[4,96,1024]{2,1,0:T(8,128)S(1)} %bitcast.19), kind=kLoop, calls=%fused_computation | loop fusion | flops 2097152 | bytes 3805184 | tf_op jit(solution)/shard_map/concatenate | solution.py:488
  8.8 76.8 %exchange.1 = (f32[2,2048,128]{2,1,0:T(8,128)}, f32[2,4,16,1024]{3,2,1,0:T(8,128)}) custom-call(s32[64,256]{1,0:T(8,128)} %bitcast.28, s32[64,256]{1,0:T(8,128)} %bitcast.29, bf16[256,256]{1,0:T(8,128)(2,1)} %slice.20.own_ref, f32[4,2,4,16,1024]{4,3,2,1,0:T(8,128)} %bitcast.20), custom_call_target="tpu_custom_call" | custom-call | flops 40000000000 | bytes 10000000 | tf_op jit(solution)/shard_map/exchange/pallas_call | solution.py:408
  85.5 1.3 %slice.23 = f32[1,256]{1,0:T(1,128)} slice(f32[128,1024]{1,0:T(8,128)} %bitcast.22), slice={[104:105], [0:256]} | slice | bytes 2048 | tf_op jit(solution)/shard_map/slice | solution.py:502
  86.8 0.8 slice.24
  87.6 1.8 %slice.22 = f32[96,1024]{1,0:T(8,128)} slice(f32[128,1024]{1,0:T(8,128)} %bitcast.24), slice={[0:96], [0:1024]} | slice | bytes 786432 | tf_op jit(solution)/shard_map/slice | solution.py:500
  89.3 0.6 reshape.43
  90.0 3.0 %copy.17 = f32[2,2048,128]{2,1,0:T(8,128)} copy(f32[2,2048,128]{2,1,0:T(8,128)} %get-tuple-element.12) | data formatting | bytes 4194304
  (1 shorter events, 0.0 us)
Async XLA Ops:
  0.6 3.4 %copy-start = (bf16[384,1024]{1,0:T(8,128)(2,1)S(1)}, bf16[384,1024]{1,0:T(8,128)(2,1)}, u32[]{:S(2)}) copy-start(bf16[384,1024]{1,0:T(8,128)(2,1)} %param.13) | copy-start | bytes 2359300
  0.6 5.1 %copy-start.3 = (bf16[256,128]{1,0:T(8,128)(2,1)S(1)}, bf16[256,128]{1,0:T(8,128)(2,1)}, u32[]{:S(2)}) copy-start(bf16[256,128]{1,0:T(8,128)(2,1)} %param.9) | copy-start | bytes 196612
  0.7 5.1 %copy-start.4 = (bf16[256,256]{1,0:T(8,128)(2,1)S(1)}, bf16[256,256]{1,0:T(8,128)(2,1)}, u32[]{:S(2)}) copy-start(bf16[256,256]{1,0:T(8,128)(2,1)} %param.8) | copy-start | bytes 393220
  2.1 4.6 %copy-start.1 = (bf16[256,1024]{1,0:T(8,128)(2,1)S(1)}, bf16[256,1024]{1,0:T(8,128)(2,1)}, u32[]{:S(2)}) copy-start(bf16[256,1024]{1,0:T(8,128)(2,1)} %param.12) | copy-start | bytes 1572868
  2.2 4.6 %copy-start.2 = (bf16[256,1024]{1,0:T(8,128)(2,1)S(1)}, bf16[256,1024]{1,0:T(8,128)(2,1)}, u32[]{:S(2)}) copy-start(bf16[256,1024]{1,0:T(8,128)(2,1)} %param.11) | copy-start | bytes 1572868
